TPU v7x, 256 devices: a whole 4x4x8 slice. The times are simulated.
256 devices in a mesh: sta: 32 (over y, x, core), tm: 8 (over z).
Axes of the slice: x: 4, y: 4, z: 8, core: 2. Of those that a mesh axis runs over, the one named last changes fastest.
Arguments:
- traces: float32 [256, 65536], P('sta', 'tm'), may hold values from -100 to 100
- station_counts: int32 [32], P('sta'), may hold values from 4 to 8
- partners: int32 [32, 3], P('sta'), may hold values from -1 to 31, as said below
Outputs:
- correlations: float32 [32, 3, 8, 8, 1024], P('sta', None, None, None, 'tm')
Inputs may be any that keep to these rules, and one draw needn't show every extreme that they name: partners[b, 0] = b; the other entries of row b are b plus distinct offsets between 1 and 3, or -1 where no pair block is listed.
All inputs are finite; a program needn't handle non-finite values.
Results may differ from a plain program's by a relative error of at most 0.0045.
Values may be sent and summed in bfloat16 or wider, within the bound.
A program may use at most 64 MiB of HBM per device.

v0:
```python
import functools
import math

import jax
import jax.numpy as jnp
import ml_dtypes
import numpy as np
from jax import lax
from jax.experimental import pallas as pl
from jax.experimental.pallas import tpu as pltpu
from jax.sharding import PartitionSpec as P

MESH = pl.DeviceIdType.MESH
F32 = jnp.float32
BF16 = jnp.bfloat16

ST = 8
FREQ = 4096
LENGTH = 2 * FREQ
BAND = 64
HALF_LAGS = 512
SLOTS = 3
REACH = 3
PAIRS = ST * ST
LIVE_ROWS = 33


def split(table):
    high = table.astype(ml_dtypes.bfloat16)
    low = (table - high.astype(np.float64)).astype(ml_dtypes.bfloat16)
    return np.stack([high, low])


def tables(window_count):
    m = np.arange(64)
    q = np.arange(128)
    taper = 0.5 - 0.5 * np.cos(np.arange(LENGTH) * (2.0 * math.pi / LENGTH))
    taper = np.repeat(taper.astype(np.float32).reshape(64, 1, 128), ST, axis=1)
    angle = 2.0 * math.pi * (np.outer(np.arange(LIVE_ROWS), m) % 64) / 64
    parts = np.concatenate([np.cos(angle), -np.sin(angle)])
    first = split(np.kron(parts, np.eye(ST)))
    angle = 2.0 * math.pi * np.outer(np.arange(64), q) / LENGTH
    turn = np.stack([np.cos(angle[:32]), np.sin(angle[:32]), np.cos(angle[32:]), np.sin(angle[32:])])
    turn = np.repeat(turn.astype(np.float32)[:, :, None, :], ST, axis=2)
    angle = 2.0 * math.pi * (np.outer(q, np.arange(BAND)) % 128) / 128
    cos, sin, none = np.cos(angle), np.sin(angle), np.zeros((128, BAND))
    second = np.concatenate(
        [
            np.concatenate([cos, none, -sin, none], axis=1),
            np.concatenate([sin, none, cos, none], axis=1),
            np.concatenate([none, cos, none, -sin], axis=1),
            np.concatenate([none, sin, none, cos], axis=1),
        ]
    )
    second = split(second)
    lane = np.arange(128)
    bins = 64 * (lane % 64)[None, :] + np.arange(32)[:, None] + 32 * (lane // 64)[None, :]
    angle = math.pi * bins / LENGTH
    shift = np.stack([np.cos(angle), np.sin(angle)]).astype(np.float32)
    shift = np.repeat(shift[:, :, None, :], ST, axis=2)
    order = bins.reshape(-1)
    weight = np.where(order == 0, 1.0, 2.0) / math.sqrt(LENGTH * window_count)
    steps = np.outer(order, 2 * np.arange(HALF_LAGS) + 1) % (2 * LENGTH)
    angle = math.pi * steps / LENGTH
    lag_cos = (weight[:, None] * np.cos(angle)).astype(ml_dtypes.bfloat16)
    lag_sin = (weight[:, None] * np.sin(angle)).astype(ml_dtypes.bfloat16)
    return taper, first, turn, second, shift, lag_cos, lag_sin


def kernel(
    n_sta,
    n_tm,
    x_hbm,
    counts,
    partners,
    tap_hbm,
    first_hbm,
    turn_hbm,
    second_hbm,
    shift_hbm,
    cos_hbm,
    sin_hbm,
    out_ref,
    xv,
    halo,
    tapv,
    firstv,
    turnv,
    secondv,
    shiftv,
    cosv,
    sinv,
    y,
    u,
    vhi,
    vlo,
    white,
    mine,
    got,
    cross0,
    cross12,
    part0,
    part12,
    recv0,
    recv12,
    load_sem,
    halo_sem,
    white_send,
    white_recv,
    p0_send,
    p0_recv,
    p12_send,
    p12_recv,
):
    b = lax.axis_index("sta")
    j = lax.axis_index("tm")
    lanes = 2 * HALF_LAGS // n_tm

    barrier = pltpu.get_barrier_semaphore()
    peers = [(b, lax.rem(j + d, n_tm)) for d in range(1, n_tm)]
    for d in range(1, REACH + 1):
        peers.append((lax.rem(b + d, n_sta), j))
        peers.append((lax.rem(b + n_sta - d, n_sta), j))
    for peer in peers:
        pl.semaphore_signal(barrier, inc=1, device_id=peer, device_id_type=MESH)

    loads = []
    for idx, (src, dst) in enumerate(
        [
            (x_hbm, xv),
            (tap_hbm, tapv),
            (first_hbm, firstv),
            (turn_hbm, turnv),
            (second_hbm, secondv),
            (shift_hbm, shiftv),
            (cos_hbm, cosv),
            (sin_hbm, sinv),
        ]
    ):
        copy = pltpu.make_async_copy(src, dst, load_sem.at[idx])
        copy.start()
        loads.append(copy)

    pl.semaphore_wait(barrier, len(peers))
    halo_copy = pltpu.make_async_remote_copy(
        src_ref=x_hbm.at[pl.ds(0, 32)],
        dst_ref=halo,
        send_sem=halo_sem.at[0],
        recv_sem=halo_sem.at[1],
        device_id=(b, lax.rem(j + n_tm - 1, n_tm)),
        device_id_type=MESH,
    )
    halo_copy.start()

    station = lax.broadcasted_iota(jnp.int32, (ST, 128), 0)
    live = (station < counts[0]).astype(F32)

    def first_step(frames):
        total = jnp.sum(jnp.sum(frames, axis=0), axis=1, keepdims=True)
        frames = (frames - (total * (1.0 / LENGTH))[None]) * tapv[...]
        frames = frames.reshape(64 * ST, 128)
        high = frames.astype(BF16)
        y[:, 0:128] = high
        y[:, 128:256] = (frames - high.astype(F32)).astype(BF16)
        both = jnp.dot(firstv[0], y[...], preferred_element_type=F32)
        u[...] = (
            both[:, 0:128]
            + both[:, 128:256]
            + jnp.dot(firstv[1], y[:, 0:128], preferred_element_type=F32)
        ).reshape(2 * LIVE_ROWS, ST, 128)

    def turned(row):
        re0, im0 = u[row], u[LIVE_ROWS + row]
        re1, im1 = u[32 - row], u[LIVE_ROWS + 32 - row]
        c0, s0, c1, s1 = turnv[0, row], turnv[1, row], turnv[2, row], turnv[3, row]
        return (
            re0 * c0 + im0 * s0,
            im0 * c0 - re0 * s0,
            re1 * c1 - im1 * s1,
            -(im1 * c1 + re1 * s1),
        )

    def second_step(w):
        for i in range(16):
            pair = zip(turned(2 * i), turned(2 * i + 1))
            for block, (upper, lower) in enumerate(pair):
                v = jnp.concatenate([upper, lower], axis=0)
                high = v.astype(BF16)
                vhi[16 * i : 16 * i + 16, 128 * block : 128 * block + 128] = high
                vlo[16 * i : 16 * i + 16, 128 * block : 128 * block + 128] = (
                    v - high.astype(F32)
                ).astype(BF16)
        spec = (
            jnp.dot(vhi[...], secondv[0], preferred_element_type=F32)
            + jnp.dot(vlo[...], secondv[0], preferred_element_type=F32)
            + jnp.dot(vhi[...], secondv[1], preferred_element_type=F32)
        )
        re = spec[:, 0:128].reshape(32, ST, 128)
        im = spec[:, 128:256].reshape(32, ST, 128)
        energy = jnp.sum(re * re + im * im, axis=0)
        energy = (energy + pltpu.roll(energy, 64, 1)) * (1.0 / BAND)
        scale = live / jnp.sqrt(energy + 1e-06)
        re = (re * scale[None]).reshape(256, 128).astype(BF16)
        im = (im * scale[None]).reshape(256, 128).astype(BF16)
        white[w, 0] = re
        white[w, 1] = im
        re = re.astype(F32).reshape(32, ST, 128)
        im = im.astype(F32).reshape(32, ST, 128)
        mine[w, 0] = re * shiftv[0] + im * shiftv[1]
        mine[w, 1] = im * shiftv[0] - re * shiftv[1]

    def send_white(w):
        copies = []
        for d in range(1, REACH + 1):
            copy = pltpu.make_async_remote_copy(
                src_ref=white.at[w],
                dst_ref=got.at[w, d - 1],
                send_sem=white_send.at[w, d - 1],
                recv_sem=white_recv.at[w, d - 1],
                device_id=(lax.rem(b + n_sta - d, n_sta), j),
                device_id_type=MESH,
            )
            copy.start()
            copies.append(copy)
        return copies

    for copy in loads[:6]:
        copy.wait()
    first_step(xv[...])
    second_step(0)
    sent = send_white(0)
    halo_copy.wait()
    inside = (j < n_tm - 1).astype(F32)
    first_step(jnp.concatenate([xv[32:64], halo[...] * inside], axis=0))
    second_step(1)
    sent += send_white(1)

    def cross_terms(others, cross, slots):
        def body(i, carry):
            rows = pl.ds(pl.multiple_of(16 * i, 16), 16)
            right = others(rows)
            for half in range(2):
                row = 2 * i + half
                at = pl.ds(pl.multiple_of(row * 128, 128), 128)
                part = slice(8 * half, 8 * half + 8)
                for s in range(0, ST, 2):
                    kept = [[], []]
                    for t in (s, s + 1):
                        left = [
                            [
                                jnp.broadcast_to(mine[w, c, row, t : t + 1, :], (ST, 128))
                                for c in range(2)
                            ]
                            for w in range(2)
                        ]
                        for slot in range(slots):
                            re, im = None, None
                            for w in range(2):
                                a_re, a_im = left[w]
                                o_re, o_im = (value[part] for value in right[slot][w])
                                new_re = a_re * o_re + a_im * o_im
                                new_im = a_im * o_re - a_re * o_im
                                re = new_re if re is None else re + new_re
                                im = new_im if im is None else im + new_im
                            kept[0].append(re)
                            kept[1].append(im)
                    for slot in range(slots):
                        at_rows = pl.ds(slot * PAIRS + s * ST, 16)
                        for c in range(2):
                            cross[c, at_rows, at] = jnp.concatenate(
                                [kept[c][slot], kept[c][slots + slot]], axis=0
                            ).astype(BF16)
            return carry

        lax.fori_loop(0, 16, body, 0)

    def lag_terms(cross, part):
        even = jnp.dot(cross[0], cosv[...], preferred_element_type=F32)
        odd = jnp.dot(cross[1], sinv[...], preferred_element_type=F32)
        later = even - odd
        earlier = even + odd
        for e in range(n_tm // 2):
            at = slice(lanes * e, lanes * e + lanes)
            part[n_tm // 2 + e] = later[:, at].astype(BF16)
            part[n_tm // 2 - 1 - e] = earlier[:, at].astype(BF16)

    def send_part(part, recv, send_sem, recv_sem):
        copies = []
        for d in range(1, n_tm):
            to = lax.rem(j + d, n_tm)
            copy = pltpu.make_async_remote_copy(
                src_ref=part.at[to],
                dst_ref=recv.at[d - 1],
                send_sem=send_sem.at[d - 1],
                recv_sem=recv_sem.at[d - 1],
                device_id=(b, to),
                device_id_type=MESH,
            )
            copy.start()
            copies.append(copy)
        return copies

    cross_terms(
        lambda rows: [[[white[w, c, rows, :].astype(F32) for c in range(2)] for w in range(2)]],
        cross0,
        1,
    )
    loads[6].wait()
    loads[7].wait()
    lag_terms(cross0, part0)
    terms0 = send_part(part0, recv0, p0_send, p0_recv)

    for copy in sent:
        copy.wait()
    takes = [
        [(partners[0, slot] == b + d).astype(F32) for d in range(1, REACH + 1)]
        for slot in range(1, SLOTS)
    ]

    def chosen(rows):
        slots = [[[None, None], [None, None]] for _ in takes]
        for w in range(2):
            for c in range(2):
                values = [got[w, d, c, rows, :].astype(F32) for d in range(REACH)]
                for slot, take in enumerate(takes):
                    slots[slot][w][c] = (
                        values[0] * take[0] + values[1] * take[1] + values[2] * take[2]
                    )
        return slots

    cross_terms(chosen, cross12, SLOTS - 1)
    lag_terms(cross12, part12)
    terms12 = send_part(part12, recv12, p12_send, p12_recv)

    row = lax.broadcasted_iota(jnp.int32, (lanes, lanes), 0)
    column = lax.broadcasted_iota(jnp.int32, (lanes, lanes), 1)
    wanted = jnp.where(j >= n_tm // 2, column, lanes - 1 - column)
    order = (row == wanted).astype(F32)

    def finish(part, recv, copies):
        total = part[j].astype(F32)
        for d, copy in enumerate(copies):
            copy.wait()
            total = total + recv[d].astype(F32)
        return jnp.dot(
            total, order, precision=lax.Precision.HIGHEST, preferred_element_type=F32
        )

    own = finish(part0, recv0, terms0)
    pair = lax.broadcasted_iota(jnp.int32, (PAIRS, lanes), 0)
    own = jnp.where((pair >> 3) == (pair & 7), 0.0, own)
    out_ref[0:PAIRS, :] = own
    out_ref[PAIRS : SLOTS * PAIRS, :] = finish(part12, recv12, terms12)


def shards(n_sta, n_tm, traces, station_counts, partners):
    x = traces.reshape(ST, 64, 128).transpose(1, 0, 2)
    consts = [jnp.asarray(table) for table in tables(2 * n_tm)]
    lanes = 2 * HALF_LAGS // n_tm
    anywhere = pl.BlockSpec(memory_space=pl.ANY)
    scalars = pl.BlockSpec(memory_space=pltpu.SMEM)
    dma = pltpu.SemaphoreType.DMA
    series = pl.pallas_call(
        functools.partial(kernel, n_sta, n_tm),
        out_shape=jax.ShapeDtypeStruct((SLOTS * PAIRS, lanes), F32),
        in_specs=[anywhere, scalars, scalars] + [anywhere] * len(consts),
        out_specs=pl.BlockSpec(memory_space=pltpu.VMEM),
        scratch_shapes=[
            pltpu.VMEM((64, ST, 128), F32),
            pltpu.VMEM((32, ST, 128), F32),
            *[pltpu.VMEM(table.shape, table.dtype) for table in consts],
            pltpu.VMEM((64 * ST, 256), BF16),
            pltpu.VMEM((2 * LIVE_ROWS, ST, 128), F32),
            pltpu.VMEM((256, 512), BF16),
            pltpu.VMEM((256, 512), BF16),
            pltpu.VMEM((2, 2, 256, 128), BF16),
            pltpu.VMEM((2, 2, 32, ST, 128), F32),
            pltpu.VMEM((2, REACH, 2, 256, 128), BF16),
            pltpu.VMEM((2, PAIRS, FREQ), BF16),
            pltpu.VMEM((2, 2 * PAIRS, FREQ), BF16),
            pltpu.VMEM((n_tm, PAIRS, lanes), BF16),
            pltpu.VMEM((n_tm, 2 * PAIRS, lanes), BF16),
            pltpu.VMEM((n_tm - 1, PAIRS, lanes), BF16),
            pltpu.VMEM((n_tm - 1, 2 * PAIRS, lanes), BF16),
            dma((8,)),
            dma((2,)),
            dma((2, REACH)),
            dma((2, REACH)),
            dma((n_tm - 1,)),
            dma((n_tm - 1,)),
            dma((n_tm - 1,)),
            dma((n_tm - 1,)),
        ],
        compiler_params=pltpu.CompilerParams(
            collective_id=0, has_side_effects=True, vmem_limit_bytes=56 * 2**20
        ),
    )(x, station_counts, partners, *consts)
    return series.reshape(1, SLOTS, ST, ST, lanes)


def solution(mesh):
    placed = (P("sta", "tm"), P("sta"), P("sta", None))
    return jax.shard_map(
        functools.partial(shards, mesh.shape["sta"], mesh.shape["tm"]),
        mesh=mesh,
        in_specs=placed,
        out_specs=P("sta", None, None, None, "tm"),
        check_vma=False,
    )
```

profile of v0, /device:TPU:30, one launch (start us, length us, event | category | flops | bytes accessed | tf_op | source)
XLA Modules:
  0.0 40.2 jit_solution(11045460035105676344)
XLA Ops:
  0.7 38.0 %shard_map.100 = f32[192,128]{1,0:T(8,128)} custom-call(f32[64,8,128]{2,1,0:T(8,128)} %bitcast.5, s32[1]{0:T(128)S(6)} %copy.12.counts, s32[1,3]{1,0:T(1,128)} %partners.1, f32[64,8,128]{2,1,0:T(8,128)} %constant.14.clone.tap_hbm, bf16[2,528,512]{2,1,0:T(8,128)(2,1)} %constant.15.clone.first_hbm, f32[4,32,8,128]{3,2,1,0:T(8,128)} %constant.16.clone.turn_hbm, ...), custom_call_target="tpu_custom_call" | custom-call | tf_op jit(solution)/shard_map/pallas_call | solution.py:363
  38.6 1.5 %copy.13 = f32[1,3,8,8,128]{4,3,2,1,0:T(8,128)} copy(f32[1,3,8,8,128]{4,3,2,1,0:T(8,128)} %bitcast.4) | data formatting | bytes 196608
where the time goes:
time: 40.3 us; the launch traced here: 40.2 us
  Pallas kernels  38 us (94%)
  local copies, waits for them, and re-layouts  1.54 us (4%)
  between operations  0.66 us (2%)
    pallas_call x1, Pallas kernels, shards(): pl.pallas_call(functools.partial(kernel, n_sta, n_tm), out_shape=jax.Shap...  38 us
    unnamed x1, local copies, waits for them, and re-layouts  1.54 us

commit v1 on v0

v1 whole, which is shorter than its diff:
```python
import functools
import math

import jax
import jax.numpy as jnp
import ml_dtypes
import numpy as np
from jax import lax
from jax.experimental import pallas as pl
from jax.experimental.pallas import tpu as pltpu
from jax.sharding import PartitionSpec as P

MESH = pl.DeviceIdType.MESH
F32 = jnp.float32
BF16 = jnp.bfloat16

ST = 8
FREQ = 4096
LENGTH = 2 * FREQ
BAND = 64
HALF_LAGS = 512
SLOTS = 3
REACH = 3
PAIRS = ST * ST
VMEM_LIMIT = 55100 * 2**10
LIVE_ROWS = 33


def split(table):
    high = table.astype(ml_dtypes.bfloat16)
    low = (table - high.astype(np.float64)).astype(ml_dtypes.bfloat16)
    return np.stack([high, low])


def tables(parts):
    m = np.arange(64)
    q = np.arange(128)
    taper = 0.5 - 0.5 * np.cos(np.arange(LENGTH) * (2.0 * math.pi / LENGTH))
    taper = np.repeat(taper.astype(np.float32).reshape(64, 1, 128), ST, axis=1)
    angle = 2.0 * math.pi * (np.outer(np.arange(LIVE_ROWS), m) % 64) / 64
    first = split(np.kron(np.concatenate([np.cos(angle), -np.sin(angle)]), np.eye(ST)))
    ids = np.arange(32)
    mirrored = np.where(ids == 0, 32, 64 - ids)
    near = 2.0 * math.pi * np.outer(ids, q) / LENGTH
    far = 2.0 * math.pi * np.outer(mirrored, q) / LENGTH
    turn = np.stack([np.cos(near), np.sin(near), np.cos(far), np.sin(far)])
    turn = np.repeat(turn.astype(np.float32)[:, :, None, :], ST, axis=2)
    k = np.arange(BAND)
    angle = 2.0 * math.pi * (np.outer(q, k) % 128) / 128
    cos, sin, none = np.cos(angle), np.sin(angle), np.zeros((128, BAND))
    back_cos, back_sin = cos[:, ::-1], sin[:, ::-1]
    second = np.concatenate(
        [
            np.concatenate([cos, none, -sin, none], axis=1),
            np.concatenate([sin, none, cos, none], axis=1),
            np.concatenate([none, back_cos, none, -back_sin], axis=1),
            np.concatenate([none, back_sin, none, back_cos], axis=1),
        ]
    )
    second = split(second)
    bins = np.concatenate(
        [64 * k[None, :] + ids[:, None], 64 * (63 - k)[None, :] + mirrored[:, None]], axis=1
    )
    angle = math.pi * bins / LENGTH
    shift = np.stack([np.cos(angle), np.sin(angle)]).astype(np.float32)
    shift = np.repeat(shift[:, :, None, :], ST, axis=2)
    band = bins[0] // BAND
    same_band = (band[:, None] == band[None, :]).astype(np.float32)
    mirror = (bins[0][:, None] + bins[0][None, :] == FREQ).astype(np.float32)
    lane_maps = np.stack([same_band, mirror])
    order = bins.reshape(-1)
    lags = np.arange(HALF_LAGS).reshape(parts // 2, -1, 2).transpose(0, 2, 1).reshape(-1)
    steps = np.outer(order, 2 * lags + 1) % (2 * LENGTH)
    weight = np.where(order == 0, 1.0, 2.0)
    lag_cos = weight[:, None] * np.cos(math.pi * steps / LENGTH)
    lag_cos = lag_cos.reshape(FREQ, 2, 256).transpose(1, 0, 2).astype(ml_dtypes.bfloat16)
    return taper, first, turn, second, shift, lane_maps, lag_cos


def kernel(
    n_sta,
    n_tm,
    x_hbm,
    counts,
    partners,
    tap_hbm,
    first_hbm,
    turn_hbm,
    second_hbm,
    shift_hbm,
    maps_hbm,
    cos_hbm,
    out_ref,
    xv,
    halo,
    tapv,
    firstv,
    turnv,
    secondv,
    shiftv,
    mapsv,
    cosv,
    y,
    u,
    vhi,
    vlo,
    white,
    mine,
    got,
    cross0,
    cross12,
    held,
    part0,
    part12,
    recv0,
    recv12,
    load_sem,
    come,
    halo_sem,
    white_send,
    white_recv,
    p0_send,
    p0_recv,
    p12_send,
    p12_recv,
):
    b = lax.axis_index("sta")
    j = lax.axis_index("tm")
    lanes = 2 * HALF_LAGS // n_tm
    group = n_tm // 2

    barrier = pltpu.get_barrier_semaphore()
    neighbours = [(b, lax.rem(j + 1, n_tm)), (b, lax.rem(j + n_tm - 1, n_tm))]
    peers = list(neighbours)
    odd = lax.rem(b, 2)
    ahead = (lax.rem(b + 2, n_sta), j)
    behind = (lax.rem(b + n_sta - 2, n_sta), j)
    sibling = (b + 1 - 2 * odd, j)
    across = (lax.rem(b + n_sta - 3 + 6 * odd, n_sta), j)
    third = (lax.rem(b + n_sta - 3 + 2 * odd, n_sta), j)
    peers += [ahead, behind, sibling, across]
    for peer in peers:
        pl.semaphore_signal(barrier, inc=1, device_id=peer, device_id_type=MESH)

    def pass_on(step):
        for neighbour in neighbours:
            pl.semaphore_signal(
                come.at[step], inc=1, device_id=neighbour, device_id_type=MESH
            )

    loads = []
    for idx, (src, dst) in enumerate(
        [
            (x_hbm, xv),
            (tap_hbm, tapv),
            (first_hbm, firstv),
            (turn_hbm, turnv),
            (second_hbm, secondv),
            (shift_hbm, shiftv),
            (maps_hbm, mapsv),
            (cos_hbm, cosv),
        ]
    ):
        loads.append(pltpu.make_async_copy(src, dst, load_sem.at[idx]))
    for copy in loads[:-1]:
        copy.start()

    loads[0].wait()
    pl.semaphore_wait(barrier, len(peers))
    halo_copy = pltpu.make_async_remote_copy(
        src_ref=xv.at[pl.ds(0, 32)],
        dst_ref=halo,
        send_sem=halo_sem.at[0],
        recv_sem=halo_sem.at[1],
        device_id=(b, lax.rem(j + n_tm - 1, n_tm)),
        device_id_type=MESH,
    )
    halo_copy.start()
    pass_on(0)
    loads[-1].start()

    station = lax.broadcasted_iota(jnp.int32, (ST, 128), 0)
    live = (station < counts[0]).astype(F32)

    def exact_dot(a, b):
        return jnp.dot(a, b, precision=lax.Precision.HIGHEST, preferred_element_type=F32)

    def first_step(frames):
        total = jnp.sum(jnp.sum(frames, axis=0), axis=1, keepdims=True)
        frames = (frames - (total * (1.0 / LENGTH))[None]) * tapv[...]
        frames = frames.reshape(64 * ST, 128)
        high = frames.astype(BF16)
        y[:, 0:128] = high
        y[:, 128:256] = (frames - high.astype(F32)).astype(BF16)
        both = jnp.dot(firstv[0], y[...], preferred_element_type=F32)
        u[...] = (
            both[:, 0:128]
            + both[:, 128:256]
            + jnp.dot(firstv[1], y[:, 0:128], preferred_element_type=F32)
        ).reshape(2 * LIVE_ROWS, ST, 128)

    def turned(row):
        re0, im0 = u[row], u[LIVE_ROWS + row]
        re1, im1 = (u[32], u[LIVE_ROWS + 32]) if row == 0 else (re0, im0)
        c0, s0, c1, s1 = turnv[0, row], turnv[1, row], turnv[2, row], turnv[3, row]
        return (
            re0 * c0 + im0 * s0,
            im0 * c0 - re0 * s0,
            re1 * c1 - im1 * s1,
            -(im1 * c1 + re1 * s1),
        )

    def mirrored_bins(value):
        return jnp.concatenate([exact_dot(value[0], mapsv[1])[None], pltpu.roll(value[1:], 64, 2)])

    def second_step(w):
        for i in range(16):
            pair = zip(turned(2 * i), turned(2 * i + 1))
            for block, (upper, lower) in enumerate(pair):
                v = jnp.concatenate([upper, lower], axis=0)
                high = v.astype(BF16)
                vhi[16 * i : 16 * i + 16, 128 * block : 128 * block + 128] = high
                vlo[16 * i : 16 * i + 16, 128 * block : 128 * block + 128] = (
                    v - high.astype(F32)
                ).astype(BF16)
        spec = (
            jnp.dot(vhi[...], secondv[0], preferred_element_type=F32)
            + jnp.dot(vlo[...], secondv[0], preferred_element_type=F32)
            + jnp.dot(vhi[...], secondv[1], preferred_element_type=F32)
        )
        re = spec[:, 0:128].reshape(32, ST, 128)
        im = spec[:, 128:256].reshape(32, ST, 128)
        energy = exact_dot(jnp.sum(re * re + im * im, axis=0), mapsv[0]) * (1.0 / BAND)
        scale = live / jnp.sqrt(energy + 1e-06)
        re = (re * scale[None]).reshape(2, 128, 128).astype(BF16)
        im = (im * scale[None]).reshape(2, 128, 128).astype(BF16)
        for part in range(2):
            white[w, part, 0] = re[part]
            white[w, part, 1] = im[part]

    def shifted(w):
        re = white[w, :, 0].astype(F32).reshape(32, ST, 128)
        im = white[w, :, 1].astype(F32).reshape(32, ST, 128)
        left = (re * shiftv[0] + im * shiftv[1], im * shiftv[0] - re * shiftv[1])
        for c in range(2):
            mine[w, c] = left[c]
            mine[w, 2 + c] = mirrored_bins(left[c])

    def start_white(w, part, place, source, to):
        copy = pltpu.make_async_remote_copy(
            src_ref=source,
            dst_ref=got.at[w, part, place],
            send_sem=white_send.at[w, part, place],
            recv_sem=white_recv.at[w, part, place],
            device_id=to,
            device_id_type=MESH,
        )
        copy.start()
        return copy

    def send_white(w):
        near = [start_white(w, part, 0, white.at[w, part], behind) for part in range(2)]
        far = [start_white(w, part, 1, white.at[w, part], third) for part in range(2)]
        return [[near[part], far[part]] for part in range(2)]

    def hand_on(w, part, copies):
        copies[part][0].wait()
        copies[part].append(start_white(w, part, 2, got.at[w, part, 0], sibling))

    for copy in loads[1:-1]:
        copy.wait()
    first_step(xv[...])
    second_step(0)
    sent0 = send_white(0)
    pl.semaphore_wait(come.at[0], 2)
    pass_on(1)
    shifted(0)
    halo_copy.wait()
    inside = (j < n_tm - 1).astype(F32)
    first_step(jnp.concatenate([xv[32:64], halo[...] * inside], axis=0))
    second_step(1)
    sent1 = send_white(1)
    pl.semaphore_wait(come.at[1], 2)
    pass_on(2)
    shifted(1)

    def cross_pair(others, cross, slots, part, i, first):
        rows = pl.ds(i * 16, 16)
        right = others(part, rows)
        for half in range(2):
            row = 16 * part + 2 * i + half
            at = pl.ds(row * 128, 128)
            own = slice(8 * half, 8 * half + 8)
            terms = []
            for slot in range(slots):
                terms.append([])
                for w in range(2):
                    values = [right[slot][w][c][own] for c in range(2)]
                    if first and part == 0 and half == 0:
                        values += [
                            jnp.dot(
                                value.astype(BF16),
                                mapsv[1].astype(BF16),
                                preferred_element_type=F32,
                            )
                            for value in values
                        ]
                    else:
                        values += [pltpu.roll(value, 64, 1) for value in values]
                    terms[slot].append(values)
            for s in range(0, ST, 2):
                kept = [[], []]
                for t in (s, s + 1):
                    left = [
                        [
                            jnp.broadcast_to(mine[w, c, row, t : t + 1, :], (ST, 128))
                            for c in range(4)
                        ]
                        for w in range(2)
                    ]
                    for slot in range(slots):
                        re, im = None, None
                        for w in range(2):
                            a_re, a_im, back_re, back_im = left[w]
                            o_re, o_im, other_re, other_im = terms[slot][w]
                            new_re = a_re * o_re + a_im * o_im
                            new_im = back_im * other_re - back_re * other_im
                            re = new_re if re is None else re + new_re
                            im = new_im if im is None else im + new_im
                        kept[0].append(re - im)
                        kept[1].append(re + im)
                for slot in range(slots):
                    for sign in range(2):
                        at_rows = pl.ds((sign * slots + slot) * PAIRS + s * ST, 16)
                        cross[at_rows, at] = jnp.concatenate(
                            [kept[sign][slot], kept[sign][slots + slot]], axis=0
                        ).astype(BF16)

    def cross_terms(others, cross, slots, part):
        for i in range(8):
            cross_pair(others, cross, slots, part, i, i == 0)

    half_bins = FREQ // 2
    place = lax.rem(j + n_tm // 4, group)
    far_half = lax.div(lax.rem(j + n_tm // 4, n_tm), group)

    def lag_sums(cross, half, part):
        at = slice(half_bins * part, half_bins * part + half_bins)
        return jnp.dot(cross[:, at], cosv[half, at, :], preferred_element_type=F32)

    def keep_part(sums, half, part):
        rows = sums.shape[0] // 2
        lane = lax.broadcasted_iota(jnp.int32, (rows, 256), 1)
        even = lax.rem(lane, lanes) < lanes // 2
        minus, plus = sums[:rows], sums[rows:]
        later = jnp.where(even, minus, plus).astype(BF16)
        earlier = jnp.where(even, plus, minus).astype(BF16)
        for e in range(n_tm // 4):
            at = slice(lanes * e, lanes * e + lanes)
            block = half * (n_tm // 4) + e
            part[group + block] = later[:, at]
            part[group - 1 - block] = earlier[:, at]

    def send_part(part, recv, send_sem, recv_sem, far):
        copies = []
        for r in range(0 if far else 1, group):
            to = lax.rem(j + n_tm - place + lax.rem(place + r, group) + (group if far else 0), n_tm)
            idx = r if far else group + r - 1
            copy = pltpu.make_async_remote_copy(
                src_ref=part.at[to],
                dst_ref=recv.at[idx],
                send_sem=send_sem.at[idx],
                recv_sem=recv_sem.at[idx],
                device_id=(b, to),
                device_id_type=MESH,
            )
            copy.start()
            copies.append(copy)
        return copies

    def own_rows(part, rows):
        return [[[white[w, part, c, rows, :].astype(F32) for c in range(2)] for w in range(2)]]

    cross_terms(own_rows, cross0, 1, 0)
    hand_on(0, 0, sent0)
    hand_on(0, 1, sent0)
    cross_terms(own_rows, cross0, 1, 1)
    loads[-1].wait()
    pl.semaphore_wait(come.at[2], 2)
    terms0 = []
    for far in (True, False):
        half = far_half if far else 1 - far_half
        keep_part(lag_sums(cross0, half, 0) + lag_sums(cross0, half, 1), half, part0)
        terms0 += send_part(part0, recv0, p0_send, p0_recv, far)

    hand_on(1, 0, sent1)
    hand_on(1, 1, sent1)
    offsets = (2, 1 + 2 * odd, 3 - 2 * odd)
    takes = [
        [(partners[slot] == b + offset).astype(F32) for offset in offsets]
        for slot in range(1, SLOTS)
    ]

    def chosen(part, rows):
        slots = [[[None, None], [None, None]] for _ in takes]
        for w in range(2):
            for c in range(2):
                values = [got[w, part, d, c, rows, :].astype(F32) for d in range(REACH)]
                for slot, take in enumerate(takes):
                    slots[slot][w][c] = (
                        values[0] * take[0] + values[1] * take[1] + values[2] * take[2]
                    )
        return slots

    for part in range(2):
        for copy in sent0[part][1:] + sent1[part][1:]:
            copy.wait()
        cross_terms(chosen, cross12, SLOTS - 1, part)
        if part == 0:
            for half in range(2):
                held[half] = lag_sums(cross12, half, 0)
    terms12 = []
    for far in (True, False):
        half = far_half if far else 1 - far_half
        keep_part(held[half] + lag_sums(cross12, half, 1), half, part12)
        terms12 += send_part(part12, recv12, p12_send, p12_recv, far)

    row = lax.broadcasted_iota(jnp.int32, (lanes, lanes), 0)
    column = lax.broadcasted_iota(jnp.int32, (lanes, lanes), 1)
    lag = jnp.where(row < lanes // 2, 2 * row, 2 * row - lanes + 1)
    lag = jnp.where(j >= group, lag, lanes - 1 - lag)
    order = (lag == column).astype(F32)

    def finish(part, recv, copies):
        total = part[j].astype(F32)
        for idx in list(range(group, n_tm - 1)) + list(range(group)):
            copies[idx].wait()
            total = total + recv[idx].astype(F32)
        return exact_dot(total, order)

    own = finish(part0, recv0, terms0)
    pair = lax.broadcasted_iota(jnp.int32, (PAIRS, lanes), 0)
    own = jnp.where((pair >> 3) == (pair & 7), 0.0, own)
    out_ref[0:PAIRS, :] = own
    out_ref[PAIRS : SLOTS * PAIRS, :] = finish(part12, recv12, terms12)


def shards(n_sta, n_tm, traces, station_counts, partners):
    x = traces.reshape(ST, 64, 128).transpose(1, 0, 2)
    consts = [jnp.asarray(table) for table in tables(n_tm)]
    lanes = 2 * HALF_LAGS // n_tm
    anywhere = pl.BlockSpec(memory_space=pl.ANY)
    scalars = pl.BlockSpec(memory_space=pltpu.SMEM)
    dma = pltpu.SemaphoreType.DMA
    series = pl.pallas_call(
        functools.partial(kernel, n_sta, n_tm),
        out_shape=jax.ShapeDtypeStruct((SLOTS * PAIRS, lanes), F32),
        in_specs=[anywhere, scalars, scalars] + [anywhere] * len(consts),
        out_specs=pl.BlockSpec(memory_space=pltpu.VMEM),
        scratch_shapes=[
            pltpu.VMEM((64, ST, 128), F32),
            pltpu.VMEM((32, ST, 128), F32),
            *[pltpu.VMEM(table.shape, table.dtype) for table in consts],
            pltpu.VMEM((64 * ST, 256), BF16),
            pltpu.VMEM((2 * LIVE_ROWS, ST, 128), F32),
            pltpu.VMEM((256, 512), BF16),
            pltpu.VMEM((256, 512), BF16),
            pltpu.VMEM((2, 2, 2, 128, 128), BF16),
            pltpu.VMEM((2, 4, 32, ST, 128), F32),
            pltpu.VMEM((2, 2, REACH, 2, 128, 128), BF16),
            pltpu.VMEM((2 * PAIRS, FREQ), BF16),
            pltpu.VMEM((4 * PAIRS, FREQ), BF16),
            pltpu.VMEM((2, 4 * PAIRS, 256), F32),
            pltpu.VMEM((n_tm, PAIRS, lanes), BF16),
            pltpu.VMEM((n_tm, 2 * PAIRS, lanes), BF16),
            pltpu.VMEM((n_tm - 1, PAIRS, lanes), BF16),
            pltpu.VMEM((n_tm - 1, 2 * PAIRS, lanes), BF16),
            dma((8,)),
            pltpu.SemaphoreType.REGULAR((n_tm // 2 - 1,)),
            dma((2,)),
            dma((2, 2, REACH)),
            dma((2, 2, REACH)),
            dma((n_tm - 1,)),
            dma((n_tm - 1,)),
            dma((n_tm - 1,)),
            dma((n_tm - 1,)),
        ],
        compiler_params=pltpu.CompilerParams(
            collective_id=0, has_side_effects=True, vmem_limit_bytes=VMEM_LIMIT
        ),
    )(x, station_counts, partners.reshape(SLOTS), *consts)
    norm = 1.0 / math.sqrt(2.0 * LENGTH * n_tm)
    return (series * norm).reshape(1, SLOTS, ST, ST, lanes)


def solution(mesh):
    placed = (P("sta", "tm"), P("sta"), P("sta", None))
    return jax.shard_map(
        functools.partial(shards, mesh.shape["sta"], mesh.shape["tm"]),
        mesh=mesh,
        in_specs=placed,
        out_specs=P("sta", None, None, None, "tm"),
        check_vma=False,
    )
```

time: 40.3 us -> 35.5 us (0.88)
  Pallas kernels: 38 us -> 33.4 us
  local copies, waits for them, and re-layouts: 1.54 us -> 0.65 us
  other arithmetic: 0 us -> 0.65 us
    pallas_call x1, Pallas kernels: 38 us -> 33.4 us  [shards(): pl.pallas_call(functools.partial(kernel, n_sta, n_tm), out_shape=jax.Shap...]
    unnamed x1 -> x2, local copies, waits for them, and re-layouts: 1.54 us -> 0.65 us
    mul x0 -> x1, other arithmetic: none -> 0.65 us  [shards(): return (series * norm).reshape(1, SLOTS, ST, ST, lanes)]
where the time goes in v1:
time: 35.5 us; the launch traced here: 35.4 us
  Pallas kernels  33.4 us (94%)
  between operations  0.67 us (2%)
  local copies, waits for them, and re-layouts  0.65 us (2%)
  other arithmetic  0.65 us (2%)
    pallas_call x1, Pallas kernels, shards(): pl.pallas_call(functools.partial(kernel, n_sta, n_tm), out_shape=jax.Shap...  33.4 us

profile of v1, /device:TPU:30, one launch (start us, length us, event | category | flops | bytes accessed | tf_op | source)
XLA Modules:
  0.0 35.4 jit_solution(1945456016007936031)
XLA Ops:
  0.7 0.0 copy-start
  0.7 0.6 %copy-done = s32[1,3]{1,0:T(1,128)S(1)} copy-done((s32[1,3]{1,0:T(1,128)S(1)}, s32[1,3]{1,0:T(1,128)}, u32[]{:S(2)}) %copy-start) | copy-done | bytes 36
  1.3 33.4 %shard_map.100 = f32[192,128]{1,0:T(8,128)S(1)} custom-call(f32[64,8,128]{2,1,0:T(8,128)} %bitcast.6, s32[1]{0:T(128)S(6)} %copy.11.counts, s32[3]{0:T(128)S(1)} %bitcast.5, f32[64,8,128]{2,1,0:T(8,128)} %constant.16.clone.tap_hbm, bf16[2,528,512]{2,1,0:T(8,128)(2,1)} %constant.17.clone.first_hbm, f32[4,32,8,128]{3,2,1,0:T(8,128)} %constant.18.clone.turn_hbm, ...), custom_call_target="tpu_custom_call" | custom-call | tf_op jit(solution)/shard_map/pallas_call | solution.py:455
  34.8 0.7 %broadcast_multiply_fusion = f32[192,128]{1,0:T(8,128)} fusion(f32[192,128]{1,0:T(8,128)S(1)} %shard_map.100), kind=kLoop, calls=%fused_computation | loop fusion | flops 24576 | bytes 196608 | tf_op jit(solution)/shard_map/mul | solution.py:493
Async XLA Ops:
  0.7 0.7 %copy-start = (s32[1,3]{1,0:T(1,128)S(1)}, s32[1,3]{1,0:T(1,128)}, u32[]{:S(2)}) copy-start(s32[1,3]{1,0:T(1,128)} %param.12) | copy-start | bytes 40

commit v2 on v1

--- a/solution.py
+++ b/solution.py
@@ -32,7 +32,7 @@
     return np.stack([high, low])
 
 
-def tables(parts):
+def tables():
     m = np.arange(64)
     q = np.arange(128)
     taper = 0.5 - 0.5 * np.cos(np.arange(LENGTH) * (2.0 * math.pi / LENGTH))
@@ -64,17 +64,12 @@
     angle = math.pi * bins / LENGTH
     shift = np.stack([np.cos(angle), np.sin(angle)]).astype(np.float32)
     shift = np.repeat(shift[:, :, None, :], ST, axis=2)
-    band = bins[0] // BAND
-    same_band = (band[:, None] == band[None, :]).astype(np.float32)
-    mirror = (bins[0][:, None] + bins[0][None, :] == FREQ).astype(np.float32)
-    lane_maps = np.stack([same_band, mirror])
     order = bins.reshape(-1)
-    lags = np.arange(HALF_LAGS).reshape(parts // 2, -1, 2).transpose(0, 2, 1).reshape(-1)
-    steps = np.outer(order, 2 * lags + 1) % (2 * LENGTH)
+    steps = np.outer(order, 2 * np.arange(HALF_LAGS) + 1) % (2 * LENGTH)
     weight = np.where(order == 0, 1.0, 2.0)
     lag_cos = weight[:, None] * np.cos(math.pi * steps / LENGTH)
     lag_cos = lag_cos.reshape(FREQ, 2, 256).transpose(1, 0, 2).astype(ml_dtypes.bfloat16)
-    return taper, first, turn, second, shift, lane_maps, lag_cos
+    return taper, first, turn, second, shift, lag_cos
 
 
 def kernel(
@@ -88,7 +83,6 @@
     turn_hbm,
     second_hbm,
     shift_hbm,
-    maps_hbm,
     cos_hbm,
     out_ref,
     xv,
@@ -98,7 +92,6 @@
     turnv,
     secondv,
     shiftv,
-    mapsv,
     cosv,
     y,
     u,
@@ -157,7 +150,6 @@
             (turn_hbm, turnv),
             (second_hbm, secondv),
             (shift_hbm, shiftv),
-            (maps_hbm, mapsv),
             (cos_hbm, cosv),
         ]
     ):
@@ -167,23 +159,29 @@
 
     loads[0].wait()
     pl.semaphore_wait(barrier, len(peers))
-    halo_copy = pltpu.make_async_remote_copy(
-        src_ref=xv.at[pl.ds(0, 32)],
-        dst_ref=halo,
-        send_sem=halo_sem.at[0],
-        recv_sem=halo_sem.at[1],
-        device_id=(b, lax.rem(j + n_tm - 1, n_tm)),
-        device_id_type=MESH,
-    )
-    halo_copy.start()
+    halo_copies = []
+    for part in range(4):
+        rows = pl.ds(8 * part, 8)
+        copy = pltpu.make_async_remote_copy(
+            src_ref=xv.at[rows],
+            dst_ref=halo.at[rows],
+            send_sem=halo_sem.at[0, part],
+            recv_sem=halo_sem.at[1, part],
+            device_id=(b, lax.rem(j + n_tm - 1, n_tm)),
+            device_id_type=MESH,
+        )
+        copy.start()
+        halo_copies.append(copy)
     pass_on(0)
-    loads[-1].start()
 
     station = lax.broadcasted_iota(jnp.int32, (ST, 128), 0)
     live = (station < counts[0]).astype(F32)
 
-    def exact_dot(a, b):
-        return jnp.dot(a, b, precision=lax.Precision.HIGHEST, preferred_element_type=F32)
+    lane = lax.broadcasted_iota(jnp.int32, (ST, 128), 1)
+    opposite = jnp.where(lane < 64, (64 - lane) & 63, 191 - lane)
+
+    def by_lane(value, index):
+        return jnp.take_along_axis(value, index, axis=1, mode="promise_in_bounds")
 
     def first_step(frames):
         total = jnp.sum(jnp.sum(frames, axis=0), axis=1, keepdims=True)
@@ -211,7 +209,8 @@
         )
 
     def mirrored_bins(value):
-        return jnp.concatenate([exact_dot(value[0], mapsv[1])[None], pltpu.roll(value[1:], 64, 2)])
+        first = jnp.where(lane == 0, 0.0, by_lane(value[0], opposite))
+        return jnp.concatenate([first[None], pltpu.roll(value[1:], 64, 2)])
 
     def second_step(w):
         for i in range(16):
@@ -230,7 +229,8 @@
         )
         re = spec[:, 0:128].reshape(32, ST, 128)
         im = spec[:, 128:256].reshape(32, ST, 128)
-        energy = exact_dot(jnp.sum(re * re + im * im, axis=0), mapsv[0]) * (1.0 / BAND)
+        energy = jnp.sum(re * re + im * im, axis=0)
+        energy = (energy + by_lane(energy, 127 - lane)) * (1.0 / BAND)
         scale = live / jnp.sqrt(energy + 1e-06)
         re = (re * scale[None]).reshape(2, 128, 128).astype(BF16)
         im = (im * scale[None]).reshape(2, 128, 128).astype(BF16)
@@ -258,10 +258,12 @@
         copy.start()
         return copy
 
-    def send_white(w):
-        near = [start_white(w, part, 0, white.at[w, part], behind) for part in range(2)]
-        far = [start_white(w, part, 1, white.at[w, part], third) for part in range(2)]
-        return [[near[part], far[part]] for part in range(2)]
+    def send_near(w):
+        return [[start_white(w, part, 0, white.at[w, part], behind)] for part in range(2)]
+
+    def send_far(w, copies):
+        for part in range(2):
+            copies[part].append(start_white(w, part, 1, white.at[w, part], third))
 
     def hand_on(w, part, copies):
         copies[part][0].wait()
@@ -271,40 +273,35 @@
         copy.wait()
     first_step(xv[...])
     second_step(0)
-    sent0 = send_white(0)
+    loads[-1].start()
+    sent0 = send_near(0)
+    send_far(0, sent0)
     pl.semaphore_wait(come.at[0], 2)
     pass_on(1)
     shifted(0)
-    halo_copy.wait()
+    for copy in halo_copies:
+        copy.wait()
     inside = (j < n_tm - 1).astype(F32)
     first_step(jnp.concatenate([xv[32:64], halo[...] * inside], axis=0))
     second_step(1)
-    sent1 = send_white(1)
+    sent1 = send_near(1)
     pl.semaphore_wait(come.at[1], 2)
     pass_on(2)
     shifted(1)
 
-    def cross_pair(others, cross, slots, part, i, first):
-        rows = pl.ds(i * 16, 16)
-        right = others(part, rows)
+    def cross_pair(others, cross, slots, windows, part, i):
+        right = others(part, slice(16 * i, 16 * i + 16), windows)
         for half in range(2):
             row = 16 * part + 2 * i + half
-            at = pl.ds(row * 128, 128)
+            at = slice(128 * row, 128 * row + 128)
             own = slice(8 * half, 8 * half + 8)
             terms = []
             for slot in range(slots):
                 terms.append([])
-                for w in range(2):
-                    values = [right[slot][w][c][own] for c in range(2)]
-                    if first and part == 0 and half == 0:
-                        values += [
-                            jnp.dot(
-                                value.astype(BF16),
-                                mapsv[1].astype(BF16),
-                                preferred_element_type=F32,
-                            )
-                            for value in values
-                        ]
+                for pair in right[slot]:
+                    values = [value[own] for value in pair]
+                    if row == 0:
+                        values += [by_lane(value, opposite) for value in values]
                     else:
                         values += [pltpu.roll(value, 64, 1) for value in values]
                     terms[slot].append(values)
@@ -316,13 +313,13 @@
                             jnp.broadcast_to(mine[w, c, row, t : t + 1, :], (ST, 128))
                             for c in range(4)
                         ]
-                        for w in range(2)
+                        for w in windows
                     ]
                     for slot in range(slots):
                         re, im = None, None
-                        for w in range(2):
-                            a_re, a_im, back_re, back_im = left[w]
-                            o_re, o_im, other_re, other_im = terms[slot][w]
+                        for mine_values, values in zip(left, terms[slot]):
+                            a_re, a_im, back_re, back_im = mine_values
+                            o_re, o_im, other_re, other_im = values
                             new_re = a_re * o_re + a_im * o_im
                             new_im = back_im * other_re - back_re * other_im
                             re = new_re if re is None else re + new_re
@@ -336,22 +333,16 @@
                             [kept[sign][slot], kept[sign][slots + slot]], axis=0
                         ).astype(BF16)
 
-    def cross_terms(others, cross, slots, part):
+    def cross_terms(others, cross, slots, windows, part):
         for i in range(8):
-            cross_pair(others, cross, slots, part, i, i == 0)
-
-    half_bins = FREQ // 2
-    place = lax.rem(j + n_tm // 4, group)
-    far_half = lax.div(lax.rem(j + n_tm // 4, n_tm), group)
-
-    def lag_sums(cross, half, part):
-        at = slice(half_bins * part, half_bins * part + half_bins)
-        return jnp.dot(cross[:, at], cosv[half, at, :], preferred_element_type=F32)
+            cross_pair(others, cross, slots, windows, part, i)
+
+    def lag_sums(cross, half):
+        return jnp.dot(cross[...], cosv[half], preferred_element_type=F32)
 
     def keep_part(sums, half, part):
         rows = sums.shape[0] // 2
-        lane = lax.broadcasted_iota(jnp.int32, (rows, 256), 1)
-        even = lax.rem(lane, lanes) < lanes // 2
+        even = (lax.broadcasted_iota(jnp.int32, (rows, 256), 1) & 1) == 0
         minus, plus = sums[:rows], sums[rows:]
         later = jnp.where(even, minus, plus).astype(BF16)
         earlier = jnp.where(even, plus, minus).astype(BF16)
@@ -361,82 +352,80 @@
             part[group + block] = later[:, at]
             part[group - 1 - block] = earlier[:, at]
 
-    def send_part(part, recv, send_sem, recv_sem, far):
+    def send_part(part, recv, send_sem, recv_sem):
         copies = []
-        for r in range(0 if far else 1, group):
-            to = lax.rem(j + n_tm - place + lax.rem(place + r, group) + (group if far else 0), n_tm)
-            idx = r if far else group + r - 1
+        for d in sorted(range(1, n_tm), key=lambda d: -min(d, n_tm - d)):
+            to = lax.rem(j + d, n_tm)
             copy = pltpu.make_async_remote_copy(
                 src_ref=part.at[to],
-                dst_ref=recv.at[idx],
-                send_sem=send_sem.at[idx],
-                recv_sem=recv_sem.at[idx],
+                dst_ref=recv.at[d - 1],
+                send_sem=send_sem.at[d - 1],
+                recv_sem=recv_sem.at[d - 1],
                 device_id=(b, to),
                 device_id_type=MESH,
             )
             copy.start()
-            copies.append(copy)
+            copies.append((d, copy))
         return copies
 
-    def own_rows(part, rows):
-        return [[[white[w, part, c, rows, :].astype(F32) for c in range(2)] for w in range(2)]]
-
-    cross_terms(own_rows, cross0, 1, 0)
+    def own_rows(part, rows, windows):
+        return [[[white[w, part, c, rows, :].astype(F32) for c in range(2)] for w in windows]]
+
+    cross_terms(own_rows, cross0, 1, (0, 1), 0)
+    send_far(1, sent1)
     hand_on(0, 0, sent0)
     hand_on(0, 1, sent0)
-    cross_terms(own_rows, cross0, 1, 1)
+    cross_terms(own_rows, cross0, 1, (0, 1), 1)
     loads[-1].wait()
     pl.semaphore_wait(come.at[2], 2)
-    terms0 = []
-    for far in (True, False):
-        half = far_half if far else 1 - far_half
-        keep_part(lag_sums(cross0, half, 0) + lag_sums(cross0, half, 1), half, part0)
-        terms0 += send_part(part0, recv0, p0_send, p0_recv, far)
-
-    hand_on(1, 0, sent1)
-    hand_on(1, 1, sent1)
+    for half in range(2):
+        keep_part(lag_sums(cross0, half), half, part0)
+    terms0 = send_part(part0, recv0, p0_send, p0_recv)
+
     offsets = (2, 1 + 2 * odd, 3 - 2 * odd)
     takes = [
         [(partners[slot] == b + offset).astype(F32) for offset in offsets]
         for slot in range(1, SLOTS)
     ]
 
-    def chosen(part, rows):
-        slots = [[[None, None], [None, None]] for _ in takes]
-        for w in range(2):
+    def chosen(part, rows, windows):
+        slots = [[] for _ in takes]
+        for w in windows:
+            pairs = [[] for _ in takes]
             for c in range(2):
                 values = [got[w, part, d, c, rows, :].astype(F32) for d in range(REACH)]
-                for slot, take in enumerate(takes):
-                    slots[slot][w][c] = (
-                        values[0] * take[0] + values[1] * take[1] + values[2] * take[2]
-                    )
+                for pair, take in zip(pairs, takes):
+                    pair.append(values[0] * take[0] + values[1] * take[1] + values[2] * take[2])
+            for slot, pair in zip(slots, pairs):
+                slot.append(pair)
         return slots
 
     for part in range(2):
-        for copy in sent0[part][1:] + sent1[part][1:]:
+        for copy in sent0[part][1:]:
             copy.wait()
-        cross_terms(chosen, cross12, SLOTS - 1, part)
-        if part == 0:
-            for half in range(2):
-                held[half] = lag_sums(cross12, half, 0)
-    terms12 = []
-    for far in (True, False):
-        half = far_half if far else 1 - far_half
-        keep_part(held[half] + lag_sums(cross12, half, 1), half, part12)
-        terms12 += send_part(part12, recv12, p12_send, p12_recv, far)
-
-    row = lax.broadcasted_iota(jnp.int32, (lanes, lanes), 0)
-    column = lax.broadcasted_iota(jnp.int32, (lanes, lanes), 1)
-    lag = jnp.where(row < lanes // 2, 2 * row, 2 * row - lanes + 1)
-    lag = jnp.where(j >= group, lag, lanes - 1 - lag)
-    order = (lag == column).astype(F32)
+        cross_terms(chosen, cross12, SLOTS - 1, (0,), part)
+    hand_on(1, 0, sent1)
+    hand_on(1, 1, sent1)
+    for half in range(2):
+        held[half] = lag_sums(cross12, half)
+    for part in range(2):
+        for copy in sent1[part][1:]:
+            copy.wait()
+        cross_terms(chosen, cross12, SLOTS - 1, (1,), part)
+    for half in range(2):
+        keep_part(held[half] + lag_sums(cross12, half), half, part12)
+    terms12 = send_part(part12, recv12, p12_send, p12_recv)
+
+    at = lax.broadcasted_iota(jnp.int32, (ST, lanes), 1)
+    at = jnp.where(j >= group, at, lanes - 1 - at)
 
     def finish(part, recv, copies):
         total = part[j].astype(F32)
-        for idx in list(range(group, n_tm - 1)) + list(range(group)):
-            copies[idx].wait()
-            total = total + recv[idx].astype(F32)
-        return exact_dot(total, order)
+        for d, copy in reversed(copies):
+            copy.wait()
+            total = total + recv[d - 1].astype(F32)
+        blocks = [by_lane(total[r : r + ST], at) for r in range(0, total.shape[0], ST)]
+        return jnp.concatenate(blocks, axis=0)
 
     own = finish(part0, recv0, terms0)
     pair = lax.broadcasted_iota(jnp.int32, (PAIRS, lanes), 0)
@@ -447,7 +436,7 @@
 
 def shards(n_sta, n_tm, traces, station_counts, partners):
     x = traces.reshape(ST, 64, 128).transpose(1, 0, 2)
-    consts = [jnp.asarray(table) for table in tables(n_tm)]
+    consts = [jnp.asarray(table) for table in tables()]
     lanes = 2 * HALF_LAGS // n_tm
     anywhere = pl.BlockSpec(memory_space=pl.ANY)
     scalars = pl.BlockSpec(memory_space=pltpu.SMEM)
@@ -475,9 +464,9 @@
             pltpu.VMEM((n_tm, 2 * PAIRS, lanes), BF16),
             pltpu.VMEM((n_tm - 1, PAIRS, lanes), BF16),
             pltpu.VMEM((n_tm - 1, 2 * PAIRS, lanes), BF16),
-            dma((8,)),
+            dma((7,)),
             pltpu.SemaphoreType.REGULAR((n_tm // 2 - 1,)),
-            dma((2,)),
+            dma((2, 4)),
             dma((2, 2, REACH)),
             dma((2, 2, REACH)),
             dma((n_tm - 1,)),

time: 35.5 us -> 34.6 us (0.975)
  Pallas kernels: 33.4 us -> 32.5 us
    pallas_call x1, Pallas kernels: 33.4 us -> 32.5 us  [shards(): pl.pallas_call(functools.partial(kernel, n_sta, n_tm), out_shape=jax.Shap...]
where the time goes in v2:
time: 34.6 us; the launch traced here: 34.5 us
  Pallas kernels  32.5 us (94%)
  between operations  0.67 us (2%)
  local copies, waits for them, and re-layouts  0.65 us (2%)
  other arithmetic  0.65 us (2%)
    pallas_call x1, Pallas kernels, shards(): pl.pallas_call(functools.partial(kernel, n_sta, n_tm), out_shape=jax.Shap...  32.5 us

profile of v2, /device:TPU:30, one launch (start us, length us, event | category | flops | bytes accessed | tf_op | source)
XLA Modules:
  0.0 34.5 jit_solution(8896348484283474010)
XLA Ops:
  0.7 0.0 copy-start
  0.7 0.6 %copy-done = s32[1,3]{1,0:T(1,128)S(1)} copy-done((s32[1,3]{1,0:T(1,128)S(1)}, s32[1,3]{1,0:T(1,128)}, u32[]{:S(2)}) %copy-start) | copy-done | bytes 36
  1.3 32.5 %shard_map.91 = f32[192,128]{1,0:T(8,128)S(1)} custom-call(f32[64,8,128]{2,1,0:T(8,128)} %bitcast.6, s32[1]{0:T(128)S(6)} %copy.10.counts, s32[3]{0:T(128)S(1)} %bitcast.5, f32[64,8,128]{2,1,0:T(8,128)} %constant.14.clone.tap_hbm, bf16[2,528,512]{2,1,0:T(8,128)(2,1)} %constant.15.clone.first_hbm, f32[4,32,8,128]{3,2,1,0:T(8,128)} %constant.16.clone.turn_hbm, ...), custom_call_target="tpu_custom_call" | custom-call | tf_op jit(solution)/shard_map/pallas_call | solution.py:444
  33.9 0.7 %broadcast_multiply_fusion = f32[192,128]{1,0:T(8,128)} fusion(f32[192,128]{1,0:T(8,128)S(1)} %shard_map.91), kind=kLoop, calls=%fused_computation | loop fusion | flops 24576 | bytes 196608 | tf_op jit(solution)/shard_map/mul | solution.py:482
Async XLA Ops:
  0.7 0.7 %copy-start = (s32[1,3]{1,0:T(1,128)S(1)}, s32[1,3]{1,0:T(1,128)}, u32[]{:S(2)}) copy-start(s32[1,3]{1,0:T(1,128)} %param.11) | copy-start | bytes 40

commit v3 on v2

--- a/solution.py
+++ b/solution.py
@@ -124,16 +124,35 @@
 
     barrier = pltpu.get_barrier_semaphore()
     neighbours = [(b, lax.rem(j + 1, n_tm)), (b, lax.rem(j + n_tm - 1, n_tm))]
-    peers = list(neighbours)
     odd = lax.rem(b, 2)
     ahead = (lax.rem(b + 2, n_sta), j)
     behind = (lax.rem(b + n_sta - 2, n_sta), j)
     sibling = (b + 1 - 2 * odd, j)
     across = (lax.rem(b + n_sta - 3 + 6 * odd, n_sta), j)
     third = (lax.rem(b + n_sta - 3 + 2 * odd, n_sta), j)
-    peers += [ahead, behind, sibling, across]
-    for peer in peers:
+    has_ahead, has_behind = b < n_sta - 2, b >= 2
+    sends = [has_behind, (odd == 1) | (b >= 4), has_ahead]
+    receives = [has_ahead, (odd == 0) | (b < n_sta - 3), has_ahead]
+    has_across = ((odd == 1) & (b < n_sta - 3)) | ((odd == 0) & (b >= 4))
+    for peer in neighbours + [sibling]:
         pl.semaphore_signal(barrier, inc=1, device_id=peer, device_id_type=MESH)
+    for there, peer in ((has_ahead, ahead), (has_behind, behind), (has_across, across)):
+        pl.when(there)(
+            functools.partial(
+                pl.semaphore_signal, barrier, inc=1, device_id=peer, device_id_type=MESH
+            )
+        )
+    arrivals = 3
+    for there in (has_ahead, has_behind, has_across):
+        arrivals = arrivals + there.astype(jnp.int32)
+
+    for place in range(REACH):
+
+        @pl.when(jnp.logical_not(receives[place]))
+        def _():
+            for w in range(2):
+                for part in range(2):
+                    got[w, part, place] = jnp.zeros((2, 128, 128), BF16)
 
     def pass_on(step):
         for neighbour in neighbours:
@@ -158,7 +177,7 @@
         copy.start()
 
     loads[0].wait()
-    pl.semaphore_wait(barrier, len(peers))
+    pl.semaphore_wait(barrier, arrivals)
     halo_copies = []
     for part in range(4):
         rows = pl.ds(8 * part, 8)
@@ -255,7 +274,7 @@
             device_id=to,
             device_id_type=MESH,
         )
-        copy.start()
+        pl.when(sends[place])(copy.start)
         return copy
 
     def send_near(w):
@@ -266,8 +285,12 @@
             copies[part].append(start_white(w, part, 1, white.at[w, part], third))
 
     def hand_on(w, part, copies):
-        copies[part][0].wait()
+        pl.when(receives[0])(copies[part][0].wait_recv)
         copies[part].append(start_white(w, part, 2, got.at[w, part, 0], sibling))
+
+    def arrive(copies):
+        for place in (1, 2):
+            pl.when(receives[place])(copies[place].wait_recv)
 
     for copy in loads[1:-1]:
         copy.wait()
@@ -401,16 +424,14 @@
         return slots
 
     for part in range(2):
-        for copy in sent0[part][1:]:
-            copy.wait()
+        arrive(sent0[part])
         cross_terms(chosen, cross12, SLOTS - 1, (0,), part)
     hand_on(1, 0, sent1)
     hand_on(1, 1, sent1)
     for half in range(2):
         held[half] = lag_sums(cross12, half)
     for part in range(2):
-        for copy in sent1[part][1:]:
-            copy.wait()
+        arrive(sent1[part])
         cross_terms(chosen, cross12, SLOTS - 1, (1,), part)
     for half in range(2):
         keep_part(held[half] + lag_sums(cross12, half), half, part12)
@@ -427,6 +448,9 @@
         blocks = [by_lane(total[r : r + ST], at) for r in range(0, total.shape[0], ST)]
         return jnp.concatenate(blocks, axis=0)
 
+    for copies in sent0 + sent1:
+        for place, copy in enumerate(copies):
+            pl.when(sends[place])(copy.wait_send)
     own = finish(part0, recv0, terms0)
     pair = lax.broadcasted_iota(jnp.int32, (PAIRS, lanes), 0)
     own = jnp.where((pair >> 3) == (pair & 7), 0.0, own)

time: 34.6 us -> 32.9 us (0.951)
  the two profiles are of different devices: /device:TPU:30 before, /device:TPU:14 now
where the time goes in v3:
time: 32.9 us; the launch traced here: 32.8 us
  Pallas kernels  30.9 us (94%)
  between operations  0.67 us (2%)
  local copies, waits for them, and re-layouts  0.65 us (2%)
  other arithmetic  0.65 us (2%)
    pallas_call x1, Pallas kernels, shards(): pl.pallas_call(functools.partial(kernel, n_sta, n_tm), out_shape=jax.Shap...  30.9 us

profile of v3, /device:TPU:14, one launch (start us, length us, event | category | flops | bytes accessed | tf_op | source)
XLA Modules:
  0.0 32.8 jit_solution(508032499089804618)
XLA Ops:
  0.7 0.0 copy-start
  0.7 0.6 %copy-done = s32[1,3]{1,0:T(1,128)S(1)} copy-done((s32[1,3]{1,0:T(1,128)S(1)}, s32[1,3]{1,0:T(1,128)}, u32[]{:S(2)}) %copy-start) | copy-done | bytes 36
  1.3 30.9 %shard_map.91 = f32[192,128]{1,0:T(8,128)S(1)} custom-call(f32[64,8,128]{2,1,0:T(8,128)} %bitcast.6, s32[1]{0:T(128)S(6)} %copy.10.counts, s32[3]{0:T(128)S(1)} %bitcast.5, f32[64,8,128]{2,1,0:T(8,128)} %constant.14.clone.tap_hbm, bf16[2,528,512]{2,1,0:T(8,128)(2,1)} %constant.15.clone.first_hbm, f32[4,32,8,128]{3,2,1,0:T(8,128)} %constant.16.clone.turn_hbm, ...), custom_call_target="tpu_custom_call" | custom-call | tf_op jit(solution)/shard_map/pallas_call | solution.py:468
  32.2 0.7 %broadcast_multiply_fusion = f32[192,128]{1,0:T(8,128)} fusion(f32[192,128]{1,0:T(8,128)S(1)} %shard_map.91), kind=kLoop, calls=%fused_computation | loop fusion | flops 24576 | bytes 196608 | tf_op jit(solution)/shard_map/mul | solution.py:506
Async XLA Ops:
  0.7 0.7 %copy-start = (s32[1,3]{1,0:T(1,128)S(1)}, s32[1,3]{1,0:T(1,128)}, u32[]{:S(2)}) copy-start(s32[1,3]{1,0:T(1,128)} %param.11) | copy-start | bytes 40

commit v4 on v3

--- a/solution.py
+++ b/solution.py
@@ -202,19 +202,21 @@
     def by_lane(value, index):
         return jnp.take_along_axis(value, index, axis=1, mode="promise_in_bounds")
 
-    def first_step(frames):
-        total = jnp.sum(jnp.sum(frames, axis=0), axis=1, keepdims=True)
-        frames = (frames - (total * (1.0 / LENGTH))[None]) * tapv[...]
-        frames = frames.reshape(64 * ST, 128)
+    def first_step(frames, begin, end):
+        frames = (frames * tapv[begin:end]).reshape((end - begin) * ST, 128)
+        at = slice(ST * begin, ST * end)
         high = frames.astype(BF16)
-        y[:, 0:128] = high
-        y[:, 128:256] = (frames - high.astype(F32)).astype(BF16)
-        both = jnp.dot(firstv[0], y[...], preferred_element_type=F32)
-        u[...] = (
+        y[at, 0:128] = high
+        y[at, 128:256] = (frames - high.astype(F32)).astype(BF16)
+        both = jnp.dot(firstv[0, :, at], y[at, :], preferred_element_type=F32)
+        return (
             both[:, 0:128]
             + both[:, 128:256]
-            + jnp.dot(firstv[1], y[:, 0:128], preferred_element_type=F32)
+            + jnp.dot(firstv[1, :, at], y[at, 0:128], preferred_element_type=F32)
         ).reshape(2 * LIVE_ROWS, ST, 128)
+
+    def total(frames):
+        return jnp.sum(jnp.sum(frames, axis=0), axis=1, keepdims=True)
 
     def turned(row):
         re0, im0 = u[row], u[LIVE_ROWS + row]
@@ -231,7 +233,7 @@
         first = jnp.where(lane == 0, 0.0, by_lane(value[0], opposite))
         return jnp.concatenate([first[None], pltpu.roll(value[1:], 64, 2)])
 
-    def second_step(w):
+    def second_step(w, rest=None):
         for i in range(16):
             pair = zip(turned(2 * i), turned(2 * i + 1))
             for block, (upper, lower) in enumerate(pair):
@@ -248,6 +250,9 @@
         )
         re = spec[:, 0:128].reshape(32, ST, 128)
         im = spec[:, 128:256].reshape(32, ST, 128)
+        if rest is not None:
+            rest = jnp.where(lane == 0, rest * (LENGTH / 4), 0.0)
+            re = jnp.concatenate([(re[0] - 2.0 * rest)[None], (re[1] + rest)[None], re[2:]])
         energy = jnp.sum(re * re + im * im, axis=0)
         energy = (energy + by_lane(energy, 127 - lane)) * (1.0 / BAND)
         scale = live / jnp.sqrt(energy + 1e-06)
@@ -294,7 +299,8 @@
 
     for copy in loads[1:-1]:
         copy.wait()
-    first_step(xv[...])
+    frames = xv[...]
+    u[...] = first_step(frames - (total(frames) * (1.0 / LENGTH))[None], 0, 64)
     second_step(0)
     loads[-1].start()
     sent0 = send_near(0)
@@ -302,11 +308,15 @@
     pl.semaphore_wait(come.at[0], 2)
     pass_on(1)
     shifted(0)
+    frames = xv[32:64]
+    mean = total(frames) * (2.0 / LENGTH)
+    u[...] = first_step(frames - mean[None], 0, 32)
     for copy in halo_copies:
         copy.wait()
     inside = (j < n_tm - 1).astype(F32)
-    first_step(jnp.concatenate([xv[32:64], halo[...] * inside], axis=0))
-    second_step(1)
+    frames = halo[...] * inside - mean[None]
+    u[...] += first_step(frames, 32, 64)
+    second_step(1, total(frames) * (1.0 / LENGTH))
     sent1 = send_near(1)
     pl.semaphore_wait(come.at[1], 2)
     pass_on(2)
@@ -316,7 +326,7 @@
         right = others(part, slice(16 * i, 16 * i + 16), windows)
         for half in range(2):
             row = 16 * part + 2 * i + half
-            at = slice(128 * row, 128 * row + 128)
+            at = slice(128 * (row - 16 * part), 128 * (row - 16 * part) + 128)
             own = slice(8 * half, 8 * half + 8)
             terms = []
             for slot in range(slots):
@@ -352,7 +362,7 @@
                 for slot in range(slots):
                     for sign in range(2):
                         at_rows = pl.ds((sign * slots + slot) * PAIRS + s * ST, 16)
-                        cross[at_rows, at] = jnp.concatenate(
+                        cross[part, at_rows, at] = jnp.concatenate(
                             [kept[sign][slot], kept[sign][slots + slot]], axis=0
                         ).astype(BF16)
 
@@ -360,8 +370,14 @@
         for i in range(8):
             cross_pair(others, cross, slots, windows, part, i)
 
-    def lag_sums(cross, half):
-        return jnp.dot(cross[...], cosv[half], preferred_element_type=F32)
+    half_bins = FREQ // 2
+
+    def lag_sums(cross, half, part):
+        at = slice(half_bins * part, half_bins * part + half_bins)
+        return jnp.dot(cross[part], cosv[half, at, :], preferred_element_type=F32)
+
+    def all_sums(cross, half):
+        return lag_sums(cross, half, 0) + lag_sums(cross, half, 1)
 
     def keep_part(sums, half, part):
         rows = sums.shape[0] // 2
@@ -402,7 +418,7 @@
     loads[-1].wait()
     pl.semaphore_wait(come.at[2], 2)
     for half in range(2):
-        keep_part(lag_sums(cross0, half), half, part0)
+        keep_part(all_sums(cross0, half), half, part0)
     terms0 = send_part(part0, recv0, p0_send, p0_recv)
 
     offsets = (2, 1 + 2 * odd, 3 - 2 * odd)
@@ -429,23 +445,26 @@
     hand_on(1, 0, sent1)
     hand_on(1, 1, sent1)
     for half in range(2):
-        held[half] = lag_sums(cross12, half)
+        held[half] = all_sums(cross12, half)
     for part in range(2):
         arrive(sent1[part])
+        if part == 1:
+            for half in range(2):
+                held[half] += lag_sums(cross12, half, 0)
         cross_terms(chosen, cross12, SLOTS - 1, (1,), part)
     for half in range(2):
-        keep_part(held[half] + lag_sums(cross12, half), half, part12)
+        keep_part(held[half] + lag_sums(cross12, half, 1), half, part12)
     terms12 = send_part(part12, recv12, p12_send, p12_recv)
 
     at = lax.broadcasted_iota(jnp.int32, (ST, lanes), 1)
     at = jnp.where(j >= group, at, lanes - 1 - at)
 
     def finish(part, recv, copies):
-        total = part[j].astype(F32)
+        series = part[j].astype(F32)
         for d, copy in reversed(copies):
             copy.wait()
-            total = total + recv[d - 1].astype(F32)
-        blocks = [by_lane(total[r : r + ST], at) for r in range(0, total.shape[0], ST)]
+            series = series + recv[d - 1].astype(F32)
+        blocks = [by_lane(series[r : r + ST], at) for r in range(0, series.shape[0], ST)]
         return jnp.concatenate(blocks, axis=0)
 
     for copies in sent0 + sent1:
@@ -481,8 +500,8 @@
             pltpu.VMEM((2, 2, 2, 128, 128), BF16),
             pltpu.VMEM((2, 4, 32, ST, 128), F32),
             pltpu.VMEM((2, 2, REACH, 2, 128, 128), BF16),
-            pltpu.VMEM((2 * PAIRS, FREQ), BF16),
-            pltpu.VMEM((4 * PAIRS, FREQ), BF16),
+            pltpu.VMEM((2, 2 * PAIRS, FREQ // 2), BF16),
+            pltpu.VMEM((2, 4 * PAIRS, FREQ // 2), BF16),
             pltpu.VMEM((2, 4 * PAIRS, 256), F32),
             pltpu.VMEM((n_tm, PAIRS, lanes), BF16),
             pltpu.VMEM((n_tm, 2 * PAIRS, lanes), BF16),

time: 32.9 us -> 32.7 us (level)
  no operation moved by 1% of the time
where the time goes in v4:
time: 32.7 us; the launch traced here: 32.6 us
  Pallas kernels  30.6 us (94%)
  between operations  0.67 us (2%)
  local copies, waits for them, and re-layouts  0.65 us (2%)
  other arithmetic  0.65 us (2%)
    pallas_call x1, Pallas kernels, shards(): pl.pallas_call(functools.partial(kernel, n_sta, n_tm), out_shape=jax.Shap...  30.6 us

profile of v4, /device:TPU:14, one launch (start us, length us, event | category | flops | bytes accessed | tf_op | source)
XLA Modules:
  0.0 32.6 jit_solution(18175932209701832031)
XLA Ops:
  0.7 0.0 copy-start
  0.7 0.6 %copy-done = s32[1,3]{1,0:T(1,128)S(1)} copy-done((s32[1,3]{1,0:T(1,128)S(1)}, s32[1,3]{1,0:T(1,128)}, u32[]{:S(2)}) %copy-start) | copy-done | bytes 36
  1.3 30.6 %shard_map.91 = f32[192,128]{1,0:T(8,128)S(1)} custom-call(f32[64,8,128]{2,1,0:T(8,128)} %bitcast.6, s32[1]{0:T(128)S(6)} %copy.10.counts, s32[3]{0:T(128)S(1)} %bitcast.5, f32[64,8,128]{2,1,0:T(8,128)} %constant.14.clone.tap_hbm, bf16[2,528,512]{2,1,0:T(8,128)(2,1)} %constant.15.clone.first_hbm, f32[4,32,8,128]{3,2,1,0:T(8,128)} %constant.16.clone.turn_hbm, ...), custom_call_target="tpu_custom_call" | custom-call | tf_op jit(solution)/shard_map/pallas_call | solution.py:487
  31.9 0.7 %broadcast_multiply_fusion = f32[192,128]{1,0:T(8,128)} fusion(f32[192,128]{1,0:T(8,128)S(1)} %shard_map.91), kind=kLoop, calls=%fused_computation | loop fusion | flops 24576 | bytes 196608 | tf_op jit(solution)/shard_map/mul | solution.py:525
Async XLA Ops:
  0.7 0.7 %copy-start = (s32[1,3]{1,0:T(1,128)S(1)}, s32[1,3]{1,0:T(1,128)}, u32[]{:S(2)}) copy-start(s32[1,3]{1,0:T(1,128)} %param.11) | copy-start | bytes 40

commit v5 on v4

--- a/solution.py
+++ b/solution.py
@@ -76,8 +76,8 @@
     n_sta,
     n_tm,
     x_hbm,
-    counts,
-    partners,
+    counts_hbm,
+    partners_hbm,
     tap_hbm,
     first_hbm,
     turn_hbm,
@@ -85,6 +85,8 @@
     shift_hbm,
     cos_hbm,
     out_ref,
+    counts,
+    partners,
     xv,
     halo,
     tapv,
@@ -164,6 +166,8 @@
     for idx, (src, dst) in enumerate(
         [
             (x_hbm, xv),
+            (counts_hbm, counts),
+            (partners_hbm, partners),
             (tap_hbm, tapv),
             (first_hbm, firstv),
             (turn_hbm, turnv),
@@ -193,6 +197,8 @@
         halo_copies.append(copy)
     pass_on(0)
 
+    loads[1].wait()
+    loads[2].wait()
     station = lax.broadcasted_iota(jnp.int32, (ST, 128), 0)
     live = (station < counts[0]).astype(F32)
 
@@ -297,7 +303,7 @@
         for place in (1, 2):
             pl.when(receives[place])(copies[place].wait_recv)
 
-    for copy in loads[1:-1]:
+    for copy in loads[3:-1]:
         copy.wait()
     frames = xv[...]
     u[...] = first_step(frames - (total(frames) * (1.0 / LENGTH))[None], 0, 64)
@@ -482,14 +488,15 @@
     consts = [jnp.asarray(table) for table in tables()]
     lanes = 2 * HALF_LAGS // n_tm
     anywhere = pl.BlockSpec(memory_space=pl.ANY)
-    scalars = pl.BlockSpec(memory_space=pltpu.SMEM)
     dma = pltpu.SemaphoreType.DMA
     series = pl.pallas_call(
         functools.partial(kernel, n_sta, n_tm),
         out_shape=jax.ShapeDtypeStruct((SLOTS * PAIRS, lanes), F32),
-        in_specs=[anywhere, scalars, scalars] + [anywhere] * len(consts),
+        in_specs=[anywhere] * (3 + len(consts)),
         out_specs=pl.BlockSpec(memory_space=pltpu.VMEM),
         scratch_shapes=[
+            pltpu.SMEM((1,), jnp.int32),
+            pltpu.SMEM((SLOTS,), jnp.int32),
             pltpu.VMEM((64, ST, 128), F32),
             pltpu.VMEM((32, ST, 128), F32),
             *[pltpu.VMEM(table.shape, table.dtype) for table in consts],
@@ -507,7 +514,7 @@
             pltpu.VMEM((n_tm, 2 * PAIRS, lanes), BF16),
             pltpu.VMEM((n_tm - 1, PAIRS, lanes), BF16),
             pltpu.VMEM((n_tm - 1, 2 * PAIRS, lanes), BF16),
-            dma((7,)),
+            dma((9,)),
             pltpu.SemaphoreType.REGULAR((n_tm // 2 - 1,)),
             dma((2, 4)),
             dma((2, 2, REACH)),

time: 32.7 us -> 32.1 us (0.982)
  Pallas kernels: 30.6 us -> 29.9 us
    pallas_call x1, Pallas kernels: 30.6 us -> 29.9 us  [shards(): pl.pallas_call(functools.partial(kernel, n_sta, n_tm), out_shape=jax.Shap...]
where the time goes in v5:
time: 32.1 us; the launch traced here: 31.9 us
  Pallas kernels  29.9 us (93%)
  between operations  0.67 us (2%)
  local copies, waits for them, and re-layouts  0.65 us (2%)
  other arithmetic  0.65 us (2%)
    pallas_call x1, Pallas kernels, shards(): pl.pallas_call(functools.partial(kernel, n_sta, n_tm), out_shape=jax.Shap...  29.9 us
    mul x1, other arithmetic, shards(): return (series * norm).reshape(1, SLOTS, ST, ST, lanes)  0.65 us
    unnamed x2, local copies, waits for them, and re-layouts  0.65 us

profile of v5, /device:TPU:14, one launch (start us, length us, event | category | flops | bytes accessed | tf_op | source)
XLA Modules:
  0.0 31.9 jit_solution(1100073664992255176)
XLA Ops:
  0.7 0.0 copy-start
  0.7 0.6 %copy-done = s32[1,3]{1,0:T(1,128)S(1)} copy-done((s32[1,3]{1,0:T(1,128)S(1)}, s32[1,3]{1,0:T(1,128)}, u32[]{:S(2)}) %copy-start) | copy-done | bytes 36
  1.3 29.9 %shard_map.91 = f32[192,128]{1,0:T(8,128)S(1)} custom-call(f32[64,8,128]{2,1,0:T(8,128)} %bitcast.6, s32[1]{0:T(128)S(6)} %copy.10.counts_hbm, s32[3]{0:T(128)S(1)} %bitcast.5, f32[64,8,128]{2,1,0:T(8,128)} %constant.14.clone.tap_hbm, bf16[2,528,512]{2,1,0:T(8,128)(2,1)} %constant.15.clone.first_hbm, f32[4,32,8,128]{3,2,1,0:T(8,128)} %constant.16.clone.turn_hbm, ...), custom_call_target="tpu_custom_call" | custom-call | tf_op jit(solution)/shard_map/pallas_call | solution.py:492
  31.2 0.7 %broadcast_multiply_fusion = f32[192,128]{1,0:T(8,128)} fusion(f32[192,128]{1,0:T(8,128)S(1)} %shard_map.91), kind=kLoop, calls=%fused_computation | loop fusion | flops 24576 | bytes 196608 | tf_op jit(solution)/shard_map/mul | solution.py:532
Async XLA Ops:
  0.7 0.7 %copy-start = (s32[1,3]{1,0:T(1,128)S(1)}, s32[1,3]{1,0:T(1,128)}, u32[]{:S(2)}) copy-start(s32[1,3]{1,0:T(1,128)} %param.11) | copy-start | bytes 40

commit v6 on v5

--- a/solution.py
+++ b/solution.py
@@ -180,7 +180,29 @@
     for copy in loads[:-1]:
         copy.start()
 
+    def tapered(frames, begin, end):
+        frames = (frames * tapv[begin:end]).reshape((end - begin) * ST, 128)
+        at = slice(ST * begin, ST * end)
+        high = frames.astype(BF16)
+        y[at, 0:128] = high
+        y[at, 128:256] = (frames - high.astype(F32)).astype(BF16)
+
+    def first_step(begin, end):
+        at = slice(ST * begin, ST * end)
+        both = jnp.dot(firstv[0, :, at], y[at, :], preferred_element_type=F32)
+        return (
+            both[:, 0:128]
+            + both[:, 128:256]
+            + jnp.dot(firstv[1, :, at], y[at, 0:128], preferred_element_type=F32)
+        ).reshape(2 * LIVE_ROWS, ST, 128)
+
+    def total(frames):
+        return jnp.sum(jnp.sum(frames, axis=0), axis=1, keepdims=True)
+
     loads[0].wait()
+    loads[3].wait()
+    frames = xv[...]
+    tapered(frames - (total(frames) * (1.0 / LENGTH))[None], 0, 64)
     pl.semaphore_wait(barrier, arrivals)
     halo_copies = []
     for part in range(4):
@@ -207,22 +229,6 @@
 
     def by_lane(value, index):
         return jnp.take_along_axis(value, index, axis=1, mode="promise_in_bounds")
-
-    def first_step(frames, begin, end):
-        frames = (frames * tapv[begin:end]).reshape((end - begin) * ST, 128)
-        at = slice(ST * begin, ST * end)
-        high = frames.astype(BF16)
-        y[at, 0:128] = high
-        y[at, 128:256] = (frames - high.astype(F32)).astype(BF16)
-        both = jnp.dot(firstv[0, :, at], y[at, :], preferred_element_type=F32)
-        return (
-            both[:, 0:128]
-            + both[:, 128:256]
-            + jnp.dot(firstv[1, :, at], y[at, 0:128], preferred_element_type=F32)
-        ).reshape(2 * LIVE_ROWS, ST, 128)
-
-    def total(frames):
-        return jnp.sum(jnp.sum(frames, axis=0), axis=1, keepdims=True)
 
     def turned(row):
         re0, im0 = u[row], u[LIVE_ROWS + row]
@@ -303,25 +309,28 @@
         for place in (1, 2):
             pl.when(receives[place])(copies[place].wait_recv)
 
-    for copy in loads[3:-1]:
-        copy.wait()
-    frames = xv[...]
-    u[...] = first_step(frames - (total(frames) * (1.0 / LENGTH))[None], 0, 64)
+    loads[4].wait()
+    u[...] = first_step(0, 64)
+    loads[5].wait()
+    loads[6].wait()
     second_step(0)
     loads[-1].start()
     sent0 = send_near(0)
     send_far(0, sent0)
     pl.semaphore_wait(come.at[0], 2)
     pass_on(1)
+    loads[7].wait()
     shifted(0)
     frames = xv[32:64]
     mean = total(frames) * (2.0 / LENGTH)
-    u[...] = first_step(frames - mean[None], 0, 32)
+    tapered(frames - mean[None], 0, 32)
+    u[...] = first_step(0, 32)
     for copy in halo_copies:
         copy.wait()
     inside = (j < n_tm - 1).astype(F32)
     frames = halo[...] * inside - mean[None]
-    u[...] += first_step(frames, 32, 64)
+    tapered(frames, 32, 64)
+    u[...] += first_step(32, 64)
     second_step(1, total(frames) * (1.0 / LENGTH))
     sent1 = send_near(1)
     pl.semaphore_wait(come.at[1], 2)

time: 32.1 us -> 32.1 us (level)
  no operation moved by 1% of the time
where the time goes in v6:
time: 32.1 us; the launch traced here: 32 us
  Pallas kernels  30.1 us (94%)
  between operations  0.67 us (2%)
  local copies, waits for them, and re-layouts  0.65 us (2%)
  other arithmetic  0.65 us (2%)
    pallas_call x1, Pallas kernels, shards(): pl.pallas_call(functools.partial(kernel, n_sta, n_tm), out_shape=jax.Shap...  30.1 us
    mul x1, other arithmetic, shards(): return (series * norm).reshape(1, SLOTS, ST, ST, lanes)  0.65 us
    unnamed x2, local copies, waits for them, and re-layouts  0.65 us

profile of v6, /device:TPU:14, one launch (start us, length us, event | category | flops | bytes accessed | tf_op | source)
XLA Modules:
  0.0 32.0 jit_solution(10437884605438732400)
XLA Ops:
  0.7 0.0 copy-start
  0.7 0.6 %copy-done = s32[1,3]{1,0:T(1,128)S(1)} copy-done((s32[1,3]{1,0:T(1,128)S(1)}, s32[1,3]{1,0:T(1,128)}, u32[]{:S(2)}) %copy-start) | copy-done | bytes 36
  1.3 30.1 %shard_map.91 = f32[192,128]{1,0:T(8,128)S(1)} custom-call(f32[64,8,128]{2,1,0:T(8,128)} %bitcast.6, s32[1]{0:T(128)S(6)} %copy.10.counts_hbm, s32[3]{0:T(128)S(1)} %bitcast.5, f32[64,8,128]{2,1,0:T(8,128)} %constant.14.clone.tap_hbm, bf16[2,528,512]{2,1,0:T(8,128)(2,1)} %constant.15.clone.first_hbm, f32[4,32,8,128]{3,2,1,0:T(8,128)} %constant.16.clone.turn_hbm, ...), custom_call_target="tpu_custom_call" | custom-call | tf_op jit(solution)/shard_map/pallas_call | solution.py:501
  31.4 0.7 %broadcast_multiply_fusion = f32[192,128]{1,0:T(8,128)} fusion(f32[192,128]{1,0:T(8,128)S(1)} %shard_map.91), kind=kLoop, calls=%fused_computation | loop fusion | flops 24576 | bytes 196608 | tf_op jit(solution)/shard_map/mul | solution.py:541
Async XLA Ops:
  0.7 0.7 %copy-start = (s32[1,3]{1,0:T(1,128)S(1)}, s32[1,3]{1,0:T(1,128)}, u32[]{:S(2)}) copy-start(s32[1,3]{1,0:T(1,128)} %param.11) | copy-start | bytes 40

commit v7 on v6

--- a/solution.py
+++ b/solution.py
@@ -431,9 +431,9 @@
     hand_on(0, 1, sent0)
     cross_terms(own_rows, cross0, 1, (0, 1), 1)
     loads[-1].wait()
-    pl.semaphore_wait(come.at[2], 2)
     for half in range(2):
         keep_part(all_sums(cross0, half), half, part0)
+    pl.semaphore_wait(come.at[2], 2)
     terms0 = send_part(part0, recv0, p0_send, p0_recv)
 
     offsets = (2, 1 + 2 * odd, 3 - 2 * odd)

time: 32.1 us -> 31.9 us (level)
  no operation moved by 1% of the time
where the time goes in v7:
time: 31.9 us; the launch traced here: 31.8 us
  Pallas kernels  29.8 us (93%)
  between operations  0.67 us (2%)
  local copies, waits for them, and re-layouts  0.65 us (2%)
  other arithmetic  0.65 us (2%)
    pallas_call x1, Pallas kernels, shards(): pl.pallas_call(functools.partial(kernel, n_sta, n_tm), out_shape=jax.Shap...  29.8 us
    mul x1, other arithmetic, shards(): return (series * norm).reshape(1, SLOTS, ST, ST, lanes)  0.65 us
    unnamed x2, local copies, waits for them, and re-layouts  0.65 us

profile of v7, /device:TPU:14, one launch (start us, length us, event | category | flops | bytes accessed | tf_op | source)
XLA Modules:
  0.0 31.8 jit_solution(17291578077476078179)
XLA Ops:
  0.7 0.0 copy-start
  0.7 0.6 %copy-done = s32[1,3]{1,0:T(1,128)S(1)} copy-done((s32[1,3]{1,0:T(1,128)S(1)}, s32[1,3]{1,0:T(1,128)}, u32[]{:S(2)}) %copy-start) | copy-done | bytes 36
  1.3 29.8 %shard_map.91 = f32[192,128]{1,0:T(8,128)S(1)} custom-call(f32[64,8,128]{2,1,0:T(8,128)} %bitcast.6, s32[1]{0:T(128)S(6)} %copy.10.counts_hbm, s32[3]{0:T(128)S(1)} %bitcast.5, f32[64,8,128]{2,1,0:T(8,128)} %constant.14.clone.tap_hbm, bf16[2,528,512]{2,1,0:T(8,128)(2,1)} %constant.15.clone.first_hbm, f32[4,32,8,128]{3,2,1,0:T(8,128)} %constant.16.clone.turn_hbm, ...), custom_call_target="tpu_custom_call" | custom-call | tf_op jit(solution)/shard_map/pallas_call | solution.py:501
  31.1 0.7 %broadcast_multiply_fusion = f32[192,128]{1,0:T(8,128)} fusion(f32[192,128]{1,0:T(8,128)S(1)} %shard_map.91), kind=kLoop, calls=%fused_computation | loop fusion | flops 24576 | bytes 196608 | tf_op jit(solution)/shard_map/mul | solution.py:541
Async XLA Ops:
  0.7 0.7 %copy-start = (s32[1,3]{1,0:T(1,128)S(1)}, s32[1,3]{1,0:T(1,128)}, u32[]{:S(2)}) copy-start(s32[1,3]{1,0:T(1,128)} %param.11) | copy-start | bytes 40
